TPU v7x, 32 devices: a whole 2x2x4 slice. The times are simulated.
32 devices in a mesh: groups: 2 (over y), depth: 16 (over z, x, core).
Axes of the slice: x: 2, y: 2, z: 4, core: 2. Of those that a mesh axis runs over, the one named last changes fastest.
Arguments:
- sources: float32 [2, 8, 8, 128], P(None, 'groups'), parts along dimension 1, may hold values from -6 to 6
- plan: int32 [8], P('groups'), parts along dimension 0, may hold values from 0 to 1023
- absorb: float32 [16, 16, 128], P('depth', 'groups'), parts along dimension 1, as said below
- labels: int32 [16, 16, 128], P('depth', 'groups'), parts along dimension 1, may hold values from 0 to 7
- region_kk: float32 [8], replicated, may hold values from 0.1 to 1
- damp_cells: int32 [256], P('groups'), parts along dimension 0, may hold values from 0 to 1023
- initial_guess: float32 [2, 8, 1024, 8, 128], P(None, 'groups', 'depth'), parts along dimension 1, may hold values from -3 to 3
Outputs:
- solution: float32 [2, 8, 1024, 8, 128], P(None, 'groups', 'depth'), parts along dimension 1
There are 2 independent parts, one for each index of `groups`. A program takes and returns all parts, laid end to end along the dimension named above; an argument that names none is the same for every part. Nothing has to cross between parts.
Inputs may be any that keep to these rules, and one draw needn't show every extreme that they name: `plan`: each source sits on one plane, counted over the whole depth. `damp_cells`: entries may repeat. `absorb`: every entry is positive.
All inputs are finite; a program needn't handle non-finite values.
Results may differ from a plain program's by a relative error of at most 0.0003.
Values sent between devices are 32-bit elements; how exact they have to be, the bound alone decides.
A program may use at most 64 MiB of HBM per device.

v0:
```python
import jax
import jax.numpy as jnp
from jax import lax
from jax.sharding import PartitionSpec as P

SLAB = 64
STEPS = 2


relax_weight = 0.8
shift_ratio = 0.5
damping = 3.0
coupling = 0.25


def with_halo(block, sides, width):
    for axis, dim in sides:
        count = lax.axis_size(axis)
        forward = [(i, i + 1) for i in range(count - 1)]
        backward = [(target, source) for source, target in forward]
        low = lax.ppermute(
            lax.slice_in_dim(block, block.shape[dim] - width, None, axis=dim), axis, forward
        )
        high = lax.ppermute(lax.slice_in_dim(block, 0, width, axis=dim), axis, backward)
        block = jnp.concatenate([low, block, high], axis=dim)
    return block


def carried_in(part, axis, combine, identity, reverse):
    count = lax.axis_size(axis)
    place = lax.axis_index(axis)
    ahead = count - 1 - place if reverse else place
    gathered = jax.tree.map(lambda a: lax.all_gather(a, axis), part)
    state = jax.tree.map(lambda a, e: jnp.zeros_like(a) + jnp.asarray(e, a.dtype), part, identity)

    def one(turn, state):
        source = count - 1 - turn if reverse else turn
        return combine(
            state, jax.tree.map(lambda a: lax.dynamic_index_in_dim(a, source, 0, False), gathered)
        )

    return lax.fori_loop(0, ahead, one, state)


def complex_mul(left, right):
    return jnp.stack(
        [left[0] * right[0] - left[1] * right[1], left[0] * right[1] + left[1] * right[0]]
    )


def lateral_sum(field):
    widths = [(0, 0)] * (field.ndim - 2) + [(1, 1), (0, 0)]
    padded = jnp.pad(field, widths)
    total = padded[..., 2:, :] + padded[..., :-2, :]
    widths = [(0, 0)] * (field.ndim - 1) + [(1, 1)]
    padded = jnp.pad(field, widths)
    return total + padded[..., 2:] + padded[..., :-2]


def neighbours(extended):
    middle = extended[:, :, 1:-1]
    return extended[:, :, 2:] + extended[:, :, :-2] + lateral_sum(middle)


def link(earlier, later):
    return (complex_mul(later[0], earlier[0]), complex_mul(later[0], earlier[1]) + later[1])


def local(sources, plan, absorb, labels, region_kk, damp_cells, initial_guess):
    position = lax.axis_index("depth")
    height = labels.shape[1]
    breadth = labels.shape[2]
    regions = jnp.arange(region_kk.shape[0])
    squared = jnp.sum(jnp.where(labels[..., None] == regions, region_kk, 0.0), axis=-1)
    cells = jnp.arange(height * breadth)
    layer = (
        jnp.any(damp_cells[:, None] == cells[None, :], axis=0)
        .astype(jnp.float32)
        .reshape(height, breadth)
    )
    diagonal_real_part = 6.0 - squared
    imag_diag = shift_ratio * squared + damping * layer
    complex_magnitude = diagonal_real_part * diagonal_real_part + imag_diag * imag_diag
    inverse = jnp.stack([diagonal_real_part / complex_magnitude, -imag_diag / complex_magnitude])
    orders = jnp.arange(SLAB + 1).astype(jnp.float32)[:, None, None]
    magnitude = jnp.exp(-orders * absorb / SLAB)
    phase_angle_sum = orders * jnp.sqrt(squared)
    powers = jnp.stack([magnitude * jnp.cos(phase_angle_sum), magnitude * jnp.sin(phase_angle_sum)])
    passage = powers[:, SLAB]
    toward_next = powers[:, :SLAB][:, ::-1][:, None]
    toward_prev = powers[:, :SLAB][:, None]
    entry_next = powers[:, 1:][:, None]
    entry_prev = powers[:, 1:][:, ::-1][:, None]
    local_plane = plan - position * SLAB
    hits = (jnp.arange(SLAB)[None, :] == local_plane[:, None]).astype(jnp.float32)
    forcing = sources[:, :, None] * hits[None, :, :, None, None]
    solution = initial_guess
    around_inverse = with_halo(inverse, (("depth", 1),), 1)
    inverse_wide = jnp.concatenate(
        [
            jnp.broadcast_to(around_inverse[:, 0:1], (2, 2, height, breadth)),
            jnp.broadcast_to(inverse, (2, SLAB, height, breadth)),
            jnp.broadcast_to(around_inverse[:, 2:3], (2, 2, height, breadth)),
        ],
        axis=1,
    )[:, None]
    for turn in range(STEPS):
        extended = with_halo(solution, (("depth", 2),), 1)
        beside_all = neighbours(extended)
        applied = jnp.stack(
            [
                diagonal_real_part * solution[0] - beside_all[0] - damping * layer * solution[1],
                diagonal_real_part * solution[1] - beside_all[1] + damping * layer * solution[0],
            ]
        )
        residual = forcing - applied
        emit_next = jnp.sum(complex_mul(toward_next, residual), axis=2)
        emit_prev = jnp.sum(complex_mul(toward_prev, residual), axis=2)
        identity = (
            jnp.stack([jnp.ones_like(passage[0]), jnp.zeros_like(passage[0])]),
            jnp.zeros_like(emit_next),
        )
        incoming_next = carried_in((passage, emit_next), "depth", link, identity, False)[1]
        incoming_prev = carried_in((passage, emit_prev), "depth", link, identity, True)[1]
        corrected_field = residual + coupling * (
            complex_mul(entry_next, incoming_next[:, :, None])
            + complex_mul(entry_prev, incoming_prev[:, :, None])
        )
        wide = with_halo(corrected_field, (("depth", 2),), 2)
        update = relax_weight * complex_mul(inverse_wide, wide)
        for inner in range(2):
            padded = jnp.pad(update, ((0, 0), (0, 0), (1, 1), (0, 0), (0, 0)))
            update = (1.0 - relax_weight) * update + relax_weight * complex_mul(
                inverse_wide, wide + neighbours(padded)
            )
        update = update[:, :, 2:-2]
        solution = solution + update
    return solution


def solution(mesh):
    return jax.shard_map(
        local,
        mesh=mesh,
        in_specs=(
            P(None, "groups", None, None),
            P("groups"),
            P("depth", "groups", None),
            P("depth", "groups", None),
            P(),
            P("groups"),
            P(None, "groups", "depth", None, None),
        ),
        out_specs=P(None, "groups", "depth", None, None),
        check_vma=False,
    )
```

profile of v0, /device:TPU:25, one launch (start us, length us, event | category | flops | bytes accessed | tf_op | source)
XLA Modules:
  0.0 239.0 jit_solution(2938973607917760691)
XLA Ops:
  1.6 3.7 %collective-permute-start = (f32[2,1,8,128]{3,2,1,0:T(8,128)S(1)}, f32[2,1,8,128]{3,2,1,0:T(8,128)S(1)}, u32[]{:S(2)}, u32[]{:S(2)}) collective-permute-start(f32[2,1,8,128]{3,2,1,0:T(8,128)S(1)} %get-tuple-element.386), channel_id=1, source_target_pairs={{0,1},{1,2},{2,3},{3,4},{4,5},{5,6},{6,7},{7,8},{8,9},{9,10},{10,1... | collective-permute-start | bytes 24584 | tf_op jit(solution)/shard_map/ppermute | solution.py:21
  5.3 1.9 collective-permute-start.1
  7.2 1.4 fusion.59
  8.6 3.4 %collective-permute-start.2 = (f32[2,4,1,8,128]{4,3,2,1,0:T(8,128)}, f32[2,4,1,8,128]{4,3,2,1,0:T(8,128)S(1)}, u32[]{:S(2)}, u32[]{:S(2)}) collective-permute-start(f32[2,4,1,8,128]{4,3,2,1,0:T(8,128)} %get-tuple-element.355), channel_id=1, source_target_pairs={{1,0},{2,1},{3,2},{4,3},{5,4},{6,5},{7,6},{8,7},{9,8},{10,9},{11,1... | collective-permute-start | bytes 98312 | tf_op jit(solution)/shard_map/ppermute | solution.py:24
  12.1 2.1 collective-permute-start.3
  14.3 1.7 fusion.49
  20.0 17.8 %all-gather = f32[32,1,8,128]{3,2,1,0:T(8,128)} all-gather(f32[2,1,8,128]{3,2,1,0:T(8,128)S(1)} %pad_maximum_fusion.11), channel_id=2, replica_groups=mesh['groups'=2,'depth'=16] {'depth'}, dimensions={0}, use_global_device_ids=true | all-gather | bytes 139264 | tf_op jit(solution)/shard_map/all_gather | solution.py:33
  43.0 20.9 %all-gather.2 = f32[32,4,8,128]{3,2,1,0:T(8,128)} all-gather(f32[2,4,8,128]{3,2,1,0:T(8,128)S(1)} %maximum_reduce_fusion.1), channel_id=4, replica_groups=mesh['groups'=2,'depth'=16] {'depth'}, dimensions={0}, use_global_device_ids=true | all-gather | bytes 557056 | tf_op jit(solution)/shard_map/all_gather | solution.py:33
  63.9 2.9 %while.53 = (s32[]{:T(128)}, f32[2,4,8,128]{3,2,1,0:T(8,128)S(1)}, s32[]{:T(128)}, f32[16,2,8,128]{3,2,1,0:T(8,128)}, f32[16,2,4,8,128]{4,3,2,1,0:T(8,128)}, /*i...) while((s32[]{:T(128)}, f32[2,4,8,128]{3,2,1,0:T(8,128)S(1)}, s32[]{:T(128)}, ...), condition=%wide.region_7.8_spmd, body=%wide.region_6.7_spmd.sunk | while | flops 40967 | bytes 188587 | solution.py:42
  66.9 38.1 %all-gather.1 = f32[32,4,8,128]{3,2,1,0:T(8,128)S(1)} all-gather(f32[2,4,8,128]{3,2,1,0:T(8,128)S(1)} %maximum_reduce_fusion), channel_id=3, replica_groups=mesh['groups'=2,'depth'=16] {'depth'}, dimensions={0}, use_global_device_ids=true | all-gather | bytes 557056 | tf_op jit(solution)/shard_map/all_gather | solution.py:33
  105.0 9.7 %while.52 = (s32[]{:T(128)}, f32[2,4,8,128]{3,2,1,0:T(8,128)S(1)}, s32[]{:T(128)}, f32[16,2,8,128]{3,2,1,0:T(8,128)}, f32[16,2,4,8,128]{4,3,2,1,0:T(8,128)S(1)}, /*index=5*/s32[]{:T(128)}, s32[]{:T(128)}, s32[]{:T(128)}, s32[]{}) while((s32[]{:T(128)}, f32[2,4,8,128]{3,2,1,0:T(8,128)S(1)}, s32[]{:T(128)}, f32[16,2,8,128]{3,2,1,0:T(8,128)}, ...), condition=%wide.region_4.5_spmd, body=%wide.region_3.4_spmd.sunk | while | flops 40966 | bytes 188567 | solution.py:42
  114.7 1.3 multiply_subtract_fusion.16
  117.0 5.4 %collective-permute-start.4 = (f32[2,4,2,8,128]{4,3,2,1,0:T(8,128)S(1)}, f32[2,4,2,8,128]{4,3,2,1,0:T(8,128)S(1)}, u32[]{:S(2)}, u32[]{:S(2)}) collective-permute-start(f32[2,4,2,8,128]{4,3,2,1,0:T(8,128)S(1)} %get-tuple-element.351), channel_id=1, source_target_pairs={{0,1},{1,2},{2,3},{3,4},{4,5},{5,6},{6,7},{7,8},{8,9},{9,10},{10,1... | collective-permute-start | bytes 196616 | tf_op jit(solution)/shard_map/ppermute | solution.py:21
  122.4 1.9 collective-permute-start.5
  124.4 3.6 %collective-permute-done.5 = f32[2,4,2,8,128]{4,3,2,1,0:T(8,128)S(1)} collective-permute-done((f32[2,4,2,8,128]{4,3,2,1,0:T(8,128)S(1)}, f32[2,4,2,8,128]{4,3,2,1,0:T(8,128)S(1)}, u32[]{:S(2)}, u32[]{:S(2)}) %collective-permute-start.5) | collective-permute-done | bytes 65568 | tf_op jit(solution)/shard_map/ppermute | solution.py:24
  128.7 1.5 fusion.4
  130.8 1.5 fusion.9
  132.5 1.3 copy-done.1
  134.3 1.9 collective-permute-start.6
  136.2 3.8 %collective-permute-start.7 = (f32[2,4,1,8,128]{4,3,2,1,0:T(8,128)S(1)}, f32[2,4,1,8,128]{4,3,2,1,0:T(8,128)S(1)}, u32[]{:S(2)}, u32[]{:S(2)}) collective-permute-start(f32[2,4,1,8,128]{4,3,2,1,0:T(8,128)S(1)} %get-tuple-element.350), channel_id=1, source_target_pairs={{0,1},{1,2},{2,3},{3,4},{4,5},{5,6},{6,7},{7,8},{8,9},{9,10},{10,1... | collective-permute-start | bytes 98312 | tf_op jit(solution)/shard_map/ppermute | solution.py:21
  144.7 1.7 multiply_subtract_fusion.13
  146.6 19.3 %all-gather.4 = f32[32,4,8,128]{3,2,1,0:T(8,128)S(1)} all-gather(f32[2,4,8,128]{3,2,1,0:T(8,128)S(1)} %maximum_reduce_fusion.3), channel_id=6, replica_groups=mesh['groups'=2,'depth'=16] {'depth'}, dimensions={0}, use_global_device_ids=true | all-gather | bytes 557056 | tf_op jit(solution)/shard_map/all_gather | solution.py:33
  165.8 1.5 while.55
  167.3 1.7 maximum_reduce_fusion.2
  169.0 30.6 %all-gather.3 = f32[32,4,8,128]{3,2,1,0:T(8,128)} all-gather(f32[2,4,8,128]{3,2,1,0:T(8,128)S(1)} %maximum_reduce_fusion.2), channel_id=5, replica_groups=mesh['groups'=2,'depth'=16] {'depth'}, dimensions={0}, use_global_device_ids=true | all-gather | bytes 557056 | tf_op jit(solution)/shard_map/all_gather | solution.py:33
  199.6 19.1 %while.54 = (s32[]{:T(128)}, f32[2,4,8,128]{3,2,1,0:T(8,128)S(1)}, s32[]{:T(128)}, f32[16,2,8,128]{3,2,1,0:T(8,128)}, f32[16,2,4,8,128]{4,3,2,1,0:T(8,128)}, /*index=5*/s32[]{:T(128)}, s32[]{:T(128)}, s32[]{:T(128)}, s32[]{}) while((s32[]{:T(128)}, f32[2,4,8,128]{3,2,1,0:T(8,128)S(1)}, s32[]{:T(128)}, f32[16,2,8,128]{3,2,1,0:T(8,128)}, ...), condition=%wide.region_10.11_spmd, body=%wide.region_9.10_spmd.sunk | while | flops 40966 | bytes 188567 | solution.py:42
  220.9 6.1 %collective-permute-start.8 = (f32[2,4,2,8,128]{4,3,2,1,0:T(8,128)S(1)}, f32[2,4,2,8,128]{4,3,2,1,0:T(8,128)S(1)}, u32[]{:S(2)}, u32[]{:S(2)}) collective-permute-start(f32[2,4,2,8,128]{4,3,2,1,0:T(8,128)S(1)} %get-tuple-element.345), channel_id=1, source_target_pairs={{0,1},{1,2},{2,3},{3,4},{4,5},{5,6},{6,7},{7,8},{8,9},{9,10},{10,1... | collective-permute-start | bytes 196616 | tf_op jit(solution)/shard_map/ppermute | solution.py:21
  227.1 1.9 collective-permute-start.9
  229.0 3.7 %collective-permute-done.9 = f32[2,4,2,8,128]{4,3,2,1,0:T(8,128)S(1)} collective-permute-done((f32[2,4,2,8,128]{4,3,2,1,0:T(8,128)S(1)}, f32[2,4,2,8,128]{4,3,2,1,0:T(8,128)S(1)}, u32[]{:S(2)}, u32[]{:S(2)}) %collective-permute-start.9) | collective-permute-done | bytes 65568 | tf_op jit(solution)/shard_map/ppermute | solution.py:24
  233.4 1.5 fusion.14
  235.5 1.5 fusion.19
  237.2 1.8 fusion.31
  (201 shorter events, 54.7 us)
Async XLA Ops:
  1.6 36.1 %collective-permute-start = (f32[2,1,8,128]{3,2,1,0:T(8,128)S(1)}, f32[2,1,8,128]{3,2,1,0:T(8,128)S(1)}, u32[]{:S(2)}, u32[]{:S(2)}) collective-permute-start(f32[2,1,8,128]{3,2,1,0:T(8,128)S(1)} %get-tuple-element.386), channel_id=1, source_target_pairs={{0,1},{1,2},{2,3},{3,4},{4,5},{5,6},{6,7},{7,8},{8,9},{9,10},{10,1... | collective-permute-start | bytes 24584 | tf_op jit(solution)/shard_map/ppermute | solution.py:21
  5.3 32.5 %collective-permute-start.1 = (f32[2,1,8,128]{3,2,1,0:T(8,128)S(1)}, f32[2,1,8,128]{3,2,1,0:T(8,128)}, u32[]{:S(2)}, u32[]{:S(2)}) collective-permute-start(f32[2,1,8,128]{3,2,1,0:T(8,128)S(1)} %get-tuple-element.386), channel_id=1, source_target_pairs={{1,0},{2,1},{3,2},{4,3},{5,4},{6,5},{7,6},{8,7},{9,8},{10,9},{11,1... | collective-permute-start | bytes 24584 | tf_op jit(solution)/shard_map/ppermute | solution.py:24
  8.6 30.7 %collective-permute-start.2 = (f32[2,4,1,8,128]{4,3,2,1,0:T(8,128)}, f32[2,4,1,8,128]{4,3,2,1,0:T(8,128)S(1)}, u32[]{:S(2)}, u32[]{:S(2)}) collective-permute-start(f32[2,4,1,8,128]{4,3,2,1,0:T(8,128)} %get-tuple-element.355), channel_id=1, source_target_pairs={{1,0},{2,1},{3,2},{4,3},{5,4},{6,5},{7,6},{8,7},{9,8},{10,9},{11,1... | collective-permute-start | bytes 98312 | tf_op jit(solution)/shard_map/ppermute | solution.py:24
  12.1 27.3 %collective-permute-start.3 = (f32[2,4,1,8,128]{4,3,2,1,0:T(8,128)S(1)}, f32[2,4,1,8,128]{4,3,2,1,0:T(8,128)S(1)}, u32[]{:S(2)}, u32[]{:S(2)}) collective-permute-start(f32[2,4,1,8,128]{4,3,2,1,0:T(8,128)S(1)} %get-tuple-element.356), channel_id=1, source_target_pairs={{0,1},{1,2},{2,3},{3,4},{4,5},{5,6},{6,7},{7,8},{8,9},{9,10},{10,1... | collective-permute-start | bytes 98312 | tf_op jit(solution)/shard_map/ppermute | solution.py:21
  14.3 2.7 %copy-start.21 = (s32[4]{0:T(128)S(1)}, s32[4]{0:T(128)}, u32[]{:S(2)}) copy-start(s32[4]{0:T(128)} %param.16) | copy-start | bytes 52
  17.0 22.4 %copy-start = (f32[2,4,64,8,128]{4,3,2,1,0:T(8,128)S(1)}, f32[2,4,64,8,128]{4,3,2,1,0:T(8,128)}, u32[]{:S(2)}) copy-start(f32[2,4,64,8,128]{4,3,2,1,0:T(8,128)} %param.21) | copy-start | bytes 6291460
  40.5 0.8 copy-start.20
  40.8 1.0 copy-start.6
  41.3 0.9 copy-start.8
  41.3 1.0 copy-start.10
  41.3 1.1 copy-start.12
  105.0 11.1 %copy-start.14 = (f32[64,8,128]{2,1,0:T(8,128)S(1)}, f32[64,8,128]{2,1,0:T(8,128)}, u32[]{:S(2)}) copy-start(f32[64,8,128]{2,1,0:T(8,128)} %get-tuple-element.368) | copy-start | bytes 786436
  105.0 11.1 %copy-start.16 = (f32[64,8,128]{2,1,0:T(8,128)S(1)}, f32[64,8,128]{2,1,0:T(8,128)}, u32[]{:S(2)}) copy-start(f32[64,8,128]{2,1,0:T(8,128)} %get-tuple-element.392) | copy-start | bytes 786436
  114.7 1.6 copy-start.7
  116.4 8.0 %copy-start.19 = (f32[2,68,8,128]{3,2,1,0:T(8,128)S(1)}, f32[2,68,8,128]{3,2,1,0:T(8,128)}, u32[]{:S(2)}) copy-start(f32[2,68,8,128]{3,2,1,0:T(8,128)} %pad_maximum_fusion.10) | copy-start | bytes 1671172
  117.0 7.4 %collective-permute-start.4 = (f32[2,4,2,8,128]{4,3,2,1,0:T(8,128)S(1)}, f32[2,4,2,8,128]{4,3,2,1,0:T(8,128)S(1)}, u32[]{:S(2)}, u32[]{:S(2)}) collective-permute-start(f32[2,4,2,8,128]{4,3,2,1,0:T(8,128)S(1)} %get-tuple-element.351), channel_id=1, source_target_pairs={{0,1},{1,2},{2,3},{3,4},{4,5},{5,6},{6,7},{7,8},{8,9},{9,10},{10,1... | collective-permute-start | bytes 196616 | tf_op jit(solution)/shard_map/ppermute | solution.py:21
  122.4 5.6 %collective-permute-start.5 = (f32[2,4,2,8,128]{4,3,2,1,0:T(8,128)S(1)}, f32[2,4,2,8,128]{4,3,2,1,0:T(8,128)S(1)}, u32[]{:S(2)}, u32[]{:S(2)}) collective-permute-start(f32[2,4,2,8,128]{4,3,2,1,0:T(8,128)S(1)} %get-tuple-element.352), channel_id=1, source_target_pairs={{1,0},{2,1},{3,2},{4,3},{5,4},{6,5},{7,6},{8,7},{9,8},{10,9},{11,1... | collective-permute-start | bytes 196616 | tf_op jit(solution)/shard_map/ppermute | solution.py:24
  132.2 1.6 copy-start.1
  134.3 5.8 %collective-permute-start.6 = (f32[2,4,1,8,128]{4,3,2,1,0:T(8,128)S(1)}, f32[2,4,1,8,128]{4,3,2,1,0:T(8,128)S(1)}, u32[]{:S(2)}, u32[]{:S(2)}) collective-permute-start(f32[2,4,1,8,128]{4,3,2,1,0:T(8,128)S(1)} %get-tuple-element.349), channel_id=1, source_target_pairs={{1,0},{2,1},{3,2},{4,3},{5,4},{6,5},{7,6},{8,7},{9,8},{10,9},{11,1... | collective-permute-start | bytes 98312 | tf_op jit(solution)/shard_map/ppermute | solution.py:24
  136.2 4.7 %collective-permute-start.7 = (f32[2,4,1,8,128]{4,3,2,1,0:T(8,128)S(1)}, f32[2,4,1,8,128]{4,3,2,1,0:T(8,128)S(1)}, u32[]{:S(2)}, u32[]{:S(2)}) collective-permute-start(f32[2,4,1,8,128]{4,3,2,1,0:T(8,128)S(1)} %get-tuple-element.350), channel_id=1, source_target_pairs={{0,1},{1,2},{2,3},{3,4},{4,5},{5,6},{6,7},{7,8},{8,9},{9,10},{10,1... | collective-permute-start | bytes 98312 | tf_op jit(solution)/shard_map/ppermute | solution.py:21
  142.3 1.0 copy-start.2
  142.3 1.3 copy-start.4
  143.6 0.9 copy-start.9
  143.6 1.0 copy-start.11
  143.6 1.1 copy-start.13
  167.3 51.4 %copy-start.18 = (f32[64,8,128]{2,1,0:T(8,128)S(1)}, f32[64,8,128]{2,1,0:T(8,128)}, u32[]{:S(2)}) copy-start(f32[64,8,128]{2,1,0:T(8,128)} %reverse_bitcast_fusion) | copy-start | bytes 786436
  199.6 20.5 %copy-start.15 = (f32[64,8,128]{2,1,0:T(8,128)S(1)}, f32[64,8,128]{2,1,0:T(8,128)}, u32[]{:S(2)}) copy-start(f32[64,8,128]{2,1,0:T(8,128)} %get-tuple-element.368) | copy-start | bytes 786436
  199.6 20.5 %copy-start.17 = (f32[64,8,128]{2,1,0:T(8,128)S(1)}, f32[64,8,128]{2,1,0:T(8,128)}, u32[]{:S(2)}) copy-start(f32[64,8,128]{2,1,0:T(8,128)} %get-tuple-element.392) | copy-start | bytes 786436
  218.7 1.6 copy-start.3
  218.7 1.6 copy-start.5
  220.9 8.1 %collective-permute-start.8 = (f32[2,4,2,8,128]{4,3,2,1,0:T(8,128)S(1)}, f32[2,4,2,8,128]{4,3,2,1,0:T(8,128)S(1)}, u32[]{:S(2)}, u32[]{:S(2)}) collective-permute-start(f32[2,4,2,8,128]{4,3,2,1,0:T(8,128)S(1)} %get-tuple-element.345), channel_id=1, source_target_pairs={{0,1},{1,2},{2,3},{3,4},{4,5},{5,6},{6,7},{7,8},{8,9},{9,10},{10,1... | collective-permute-start | bytes 196616 | tf_op jit(solution)/shard_map/ppermute | solution.py:21
  227.1 5.7 %collective-permute-start.9 = (f32[2,4,2,8,128]{4,3,2,1,0:T(8,128)S(1)}, f32[2,4,2,8,128]{4,3,2,1,0:T(8,128)S(1)}, u32[]{:S(2)}, u32[]{:S(2)}) collective-permute-start(f32[2,4,2,8,128]{4,3,2,1,0:T(8,128)S(1)} %get-tuple-element.346), channel_id=1, source_target_pairs={{1,0},{2,1},{3,2},{4,3},{5,4},{6,5},{7,6},{8,7},{9,8},{10,9},{11,1... | collective-permute-start | bytes 196616 | tf_op jit(solution)/shard_map/ppermute | solution.py:24
where the time goes:
time: 242 us; the launch traced here: 239 us
  blocking collectives  127 us (52%)
  other arithmetic  39.2 us (16%)
  starting transfers between devices  32.3 us (13%)
  local copies, waits for them, and re-layouts  31.5 us (13%)
  waiting for transfers between devices  8.14 us (3%)
    all_gather x5, blocking collectives, carried_in(): gathered = jax.tree.map(lambda a: lax.all_gather(a, axis), part)  127 us
    mul x37, local copies, waits for them, and re-layouts, complex_mul(): left[0] * right[0] - left[1] * right[1]  22.3 us
    ppermute x5, starting transfers between devices, with_halo(): lax.ppermute(lax.slice_in_dim(block, block.shape[dim] - width, None, axis...  21.2 us
    add x30, other arithmetic, link(): complex_mul(later[0], earlier[1]) + later[1]  11.7 us
    ppermute x5, starting transfers between devices, with_halo(): lax.ppermute(lax.slice_in_dim(block, 0, width, axis=dim), axis, backward)  11.1 us
    ppermute x5, waiting for transfers between devices, with_halo(): lax.ppermute(lax.slice_in_dim(block, 0, width, axis=dim), axis, backward)  7.32 us
    sub x42, other arithmetic, complex_mul(): left[0] * right[0] - left[1] * right[1]  7.17 us
    add x4, other arithmetic, local(): wide + neighbours(padded)  5.84 us
  transfers between devices with their start and end apart: 10, of which 3 were waited for; matrix products, arithmetic and copies ran while one was open for 4% of the time, Pallas kernels for 0%

commit v1 on v0

v1 whole, which is shorter than its diff:
```python
import functools

import jax
import jax.numpy as jnp
from jax import lax
from jax.experimental import pallas as pl
from jax.experimental.pallas import tpu as pltpu
from jax.sharding import PartitionSpec as P

STEPS = 2
HALO = 3 * STEPS
CHUNK = 8

relax_weight = 0.8
shift_ratio = 0.5
damping = 3.0
coupling = 0.25


def cmul(a, b):
    return (a[0] * b[0] - a[1] * b[1], a[0] * b[1] + a[1] * b[0])


def cadd(a, b):
    return (a[0] + b[0], a[1] + b[1])


def kernel(
    n, chains_of, sources, plan, absorb, labels, kk, damp, guess, out,
    field, work, inner, power, side_next, side_prev, own, side, emits, gathered, scanned,
    incoming, passages, local_sem, halo_send, halo_recv, side_send, side_recv, pass_send,
    pass_recv, emit_send, emit_recv, scan_send, scan_recv, out_sem,
):
    me = lax.axis_index("depth")
    count = guess.shape[1]
    slab = guess.shape[2]
    height, breadth = guess.shape[3:]
    wing = HALO - 1
    chains = 2 * count

    def owner(chain):
        return (chain * n) // chains

    def slot(chain):
        return 0 if chains_of == 1 else chain

    owners = sorted({(c * n) // chains for c in range(chains)})

    barrier = pltpu.get_barrier_semaphore()

    def greet(i, _):
        pl.semaphore_signal(
            barrier, inc=1, device_id={"depth": lax.rem(me + i, n)},
            device_id_type=pl.DeviceIdType.MESH,
        )
        return 0

    lax.fori_loop(1, n, greet, 0)

    def load(s):
        return pltpu.make_async_copy(
            guess.at[:, s], field.at[s, :, pl.ds(HALO, slab)], local_sem.at[s]
        )

    for s in range(count):
        load(s).start()

    label = labels[0]
    squared = jnp.zeros((height, breadth), jnp.float32)
    for r in range(kk.shape[0]):
        squared = squared + jnp.where(label == r, kk[r], 0.0)
    rows = lax.broadcasted_iota(jnp.int32, (height, breadth), 0)
    lanes = lax.broadcasted_iota(jnp.int32, (height, breadth), 1)
    number = rows * breadth + lanes

    def mark(i, layer):
        return jnp.where(number == damp[i], 1.0, layer)

    layer = lax.fori_loop(
        0, damp.shape[0], mark, jnp.zeros((height, breadth), jnp.float32), unroll=8
    )
    own[0] = squared
    own[1] = absorb[0]

    pl.semaphore_wait(barrier, n - 1)

    def remote(src, dst, send, recv, target):
        return pltpu.make_async_remote_copy(
            src_ref=src, dst_ref=dst, send_sem=send, recv_sem=recv,
            device_id={"depth": target}, device_id_type=pl.DeviceIdType.MESH,
        )

    def side_copy(direction):
        return remote(
            own, side.at[1 - direction], side_send.at[direction], side_recv.at[1 - direction],
            me + (2 * direction - 1),
        )

    def halo_copy(s, direction):
        first = slab - HALO if direction else 0
        landing = 0 if direction else slab + HALO
        return remote(
            guess.at[:, s, pl.ds(first, HALO)], field.at[s, :, pl.ds(landing, HALO)],
            halo_send.at[s, direction], halo_recv.at[s, 1 - direction],
            me + (2 * direction - 1),
        )

    has = (me > 0, me < n - 1)
    for direction in range(2):
        @pl.when(has[direction])
        def _():
            side_copy(direction).start()
            for s in range(count):
                halo_copy(s, direction).start()

        @pl.when(jnp.logical_not(has[direction]))
        def _():
            side[direction] = jnp.zeros_like(side[direction])
            landing = slab + HALO if direction else 0
            for s in range(count):
                field[s, :, pl.ds(landing, HALO)] = jnp.zeros(
                    (2, HALO, height, breadth), jnp.float32
                )

    def wave(sq, ab):
        magnitude = jnp.exp(-ab / slab)
        phase = jnp.sqrt(sq)
        return (magnitude * jnp.cos(phase), magnitude * jnp.sin(phase))

    def relaxer(sq):
        real = 6.0 - sq
        imag = shift_ratio * sq + damping * layer
        size = real * real + imag * imag
        return (relax_weight * (real / size), relax_weight * (-imag / size))

    a_own = wave(squared, absorb[0])
    table = {0: (jnp.ones_like(squared), jnp.zeros_like(squared)), 1: a_own}
    power[0, 0], power[1, 0] = table[0]
    power[0, 1], power[1, 1] = a_own
    top = 1
    while top < slab:
        more = min(top, slab - top)
        head = (power[0, top], power[1, top])
        for j in range(1, more + 1):
            power[0, top + j], power[1, top + j] = cmul(head, (power[0, j], power[1, j]))
        top += more
    passage = (power[0, slab], power[1, slab])

    def pass_copy(i):
        return remote(
            power.at[:, slab], passages.at[me], pass_send.at[i], pass_recv, owners[i]
        )

    for i, target in enumerate(owners):
        @pl.when(me != target)
        def _():
            pass_copy(i).start()

        @pl.when(me == target)
        def _():
            passages[me, 0], passages[me, 1] = passage

    for direction in range(2):
        @pl.when(has[direction])
        def _():
            side_copy(1 - direction).wait_recv()

    damped = damping * layer
    real_own = 6.0 - squared
    g_own = relaxer(squared)
    media = []
    for direction in range(2):
        sq = side[direction, 0]
        inside = jnp.where(has[direction], 1.0, 0.0)
        g = relaxer(sq)
        a = wave(sq, side[direction, 1])

        def raised(k, a=a):
            total = None
            base = a
            while k:
                if k & 1:
                    total = base if total is None else cmul(total, base)
                k >>= 1
                if k:
                    base = cmul(base, base)
            return total

        low = a
        high = raised(slab - wing + 1)
        for i in range(wing):
            if direction == 0:
                side_next[0, 0, i], side_next[0, 1, i] = high
                side_prev[0, 0, wing - 1 - i], side_prev[0, 1, wing - 1 - i] = low
            else:
                side_next[1, 0, i], side_next[1, 1, i] = low
                side_prev[1, 0, wing - 1 - i], side_prev[1, 1, wing - 1 - i] = high
            low = cmul(low, a)
            high = cmul(high, a)
        media.append((6.0 - sq, (inside * g[0], inside * g[1])))

    keep_up, keep_down = rows > 0, rows < height - 1
    keep_left, keep_right = lanes > 0, lanes < breadth - 1

    def lateral(x):
        up = jnp.where(keep_up, pltpu.roll(x, 1, 0), 0.0)
        down = jnp.where(keep_down, pltpu.roll(x, height - 1, 0), 0.0)
        left = jnp.where(keep_left, pltpu.roll(x, 1, 1), 0.0)
        right = jnp.where(keep_right, pltpu.roll(x, breadth - 1, 1), 0.0)
        return (up + down) + (left + right)

    def window(ref, lead, first, planes):
        return [
            [ref[lead + (c, first - 1 + j)] for j in range(planes + 2)] for c in range(2)
        ]

    def beside(win, j):
        return tuple(w[j] + w[j + 2] + lateral(w[j + 1]) for w in win)

    def residual_pass(s, first, planes, real, tally):
        win = window(field, (s,), first + HALO, planes)
        source = (sources[0, s], sources[1, s])
        spot = plan[s] - me * slab
        for j in range(planes):
            value = (win[0][j + 1], win[1][j + 1])
            near = beside(win, j)
            hit = jnp.where(spot == first + j, 1.0, 0.0)
            res = (
                hit * source[0] + (near[0] - real * value[0] + damped * value[1]),
                hit * source[1] + (near[1] - real * value[1] - damped * value[0]),
            )
            work[s, 0, first + HALO + j] = res[0]
            work[s, 1, first + HALO + j] = res[1]
            if tally is not None:
                forward, backward = tally
                forward = cadd(cmul(a_own, forward), res)
                backward = cadd(
                    backward, cmul((power[0, first + j], power[1, first + j]), res)
                )
                tally = (forward, backward)
        return tally

    def start_pass(s, first, planes, g, toward, from_low, from_high):
        for j in range(planes):
            at = first + HALO + j
            up, down = toward(first + j)
            c = cadd(
                (work[s, 0, at], work[s, 1, at]), cadd(cmul(up, from_low), cmul(down, from_high))
            )
            work[s, 0, at], work[s, 1, at] = cmul(g, c)

    def middle_pass(s, first, planes, g):
        win = window(work, (s,), first + HALO, planes)
        for j in range(planes):
            at = first + HALO + j
            moved = cmul(g, beside(win, j))
            for c in range(2):
                inner[c, at] = (2.0 - relax_weight) * win[c][j + 1] + moved[c]

    def last_pass(s, first, planes, g):
        win = window(inner, (), first + HALO, planes)
        for j in range(planes):
            at = first + HALO + j
            moved = cmul(g, beside(win, j))
            for c in range(2):
                field[s, c, at] = field[s, c, at] + (
                    (1.0 - relax_weight) * win[c][j + 1] + work[s, c, at] + moved[c]
                )

    def emit_copy(t, chain):
        return remote(
            emits.at[t, chain], gathered.at[t, slot(chain), me], emit_send.at[t, chain],
            emit_recv.at[t, slot(chain)], owner(chain),
        )

    def scan_copy(t, s, direction, target):
        here = slot(2 * s + direction)
        return remote(
            scanned.at[t, here, pl.ds(target, 2)], incoming.at[t, s, direction],
            scan_send.at[t, here, target], scan_recv.at[t, s, direction], target,
        )

    def own_scan(t, s):
        for direction in range(2):
            chain = 2 * s + direction
            here = slot(chain)

            @pl.when(me == owner(chain))
            def _():
                if n > 1:
                    every = gathered.at[t, here, pl.ds(0, n - 1)]
                    pltpu.make_async_copy(every, every, emit_recv.at[t, here]).wait()
                zero = jnp.zeros((height, breadth), jnp.float32)
                edge = direction * n
                scanned[t, here, edge, 0] = zero
                scanned[t, here, edge, 1] = zero

                def one(i, state):
                    at = n - 1 - i if direction else i
                    to = at + 1 - direction
                    scanned[t, here, to, 0] = state[0]
                    scanned[t, here, to, 1] = state[1]
                    return cadd(
                        cmul((passages[at, 0], passages[at, 1]), state),
                        (gathered[t, here, at, 0], gathered[t, here, at, 1]),
                    )

                lax.fori_loop(0, n, one, (zero, zero), unroll=4)

                def give(i, _):
                    scan_copy(t, s, direction, lax.rem(me + i, n)).start()
                    return 0

                lax.fori_loop(1, n, give, 0)
                incoming[t, s, direction] = scanned[t, here, pl.ds(me, 2)]

    pieces = slab // CHUNK
    for t in range(STEPS):
        reach = 3 * (STEPS - t)

        def first_half(s, _):
            if t == 0:
                load(s).wait()
                for direction in range(2):
                    @pl.when(has[direction])
                    def _():
                        halo_copy(s, 1 - direction).wait_recv()
            zero = jnp.zeros((height, breadth), jnp.float32)
            tally = lax.fori_loop(
                0, pieces,
                lambda i, tally: residual_pass(s, i * CHUNK, CHUNK, real_own, tally),
                ((zero, zero), (zero, zero)),
            )
            for direction in range(2):
                chain = 2 * s + direction
                emits[t, chain, 0], emits[t, chain, 1] = tally[direction]

                @pl.when(me != owner(chain))
                def _():
                    emit_copy(t, chain).start()

                @pl.when(me == owner(chain))
                def _():
                    gathered[t, slot(chain), me, 0] = tally[direction][0]
                    gathered[t, slot(chain), me, 1] = tally[direction][1]
            residual_pass(s, 1 - reach, reach - 1, media[0][0], None)
            residual_pass(s, slab, reach - 1, media[1][0], None)

            @pl.when(s > 0)
            def _():
                own_scan_or_first(t, s - 1)
            return 0

        def own_scan_or_first(t, s):
            if t == 0:
                @pl.when(s == 0)
                def _():
                    for target in owners:
                        @pl.when(me == target)
                        def _():
                            if n > 1:
                                every = passages.at[pl.ds(0, n - 1)]
                                pltpu.make_async_copy(every, every, pass_recv).wait()
            own_scan(t, s)

        lax.fori_loop(0, count, first_half, 0)
        own_scan_or_first(t, jnp.int32(count - 1))

        def second_half(s, _):
            for direction in range(2):
                @pl.when(me != owner(2 * s + direction))
                def _():
                    scan_copy(t, s, direction, me).wait_recv()

            def arrived(direction, i):
                return (incoming[t, s, direction, i, 0], incoming[t, s, direction, i, 1])

            def emitted(direction):
                return (emits[t, 2 * s + direction, 0], emits[t, 2 * s + direction, 1])

            def scaled(z):
                return (coupling * z[0], coupling * z[1])

            next_low, next_own = arrived(0, 0), arrived(0, 1)
            prev_own, prev_high = arrived(1, 0), arrived(1, 1)
            next_high = scaled(cadd(cmul(passage_now(), next_own), emitted(0)))
            prev_low = scaled(cadd(cmul(passage_now(), prev_own), emitted(1)))
            next_low, next_own = scaled(next_low), scaled(next_own)
            prev_own, prev_high = scaled(prev_own), scaled(prev_high)

            def toward_own(k):
                return (
                    (power[0, k + 1], power[1, k + 1]),
                    (power[0, slab - k], power[1, slab - k]),
                )

            def toward_side(direction):
                def get(k):
                    i = k - slab if direction else k + wing
                    return (
                        (side_next[direction, 0, i], side_next[direction, 1, i]),
                        (side_prev[direction, 0, i], side_prev[direction, 1, i]),
                    )
                return get

            g_low, g_high = media[0][1], media[1][1]

            def walk(body):
                lax.fori_loop(0, pieces, lambda i, _: (body(i * CHUNK), 0)[1], 0)

            walk(lambda k: start_pass(s, k, CHUNK, g_own, toward_own, next_own, prev_own))
            start_pass(s, 1 - reach, reach - 1, g_low, toward_side(0), next_low, prev_low)
            start_pass(s, slab, reach - 1, g_high, toward_side(1), next_high, prev_high)
            walk(lambda k: middle_pass(s, k, CHUNK, g_own))
            middle_pass(s, 2 - reach, reach - 2, g_low)
            middle_pass(s, slab, reach - 2, g_high)
            walk(lambda k: last_pass(s, k, CHUNK, g_own))
            if reach > 3:
                last_pass(s, 3 - reach, reach - 3, g_low)
                last_pass(s, slab, reach - 3, g_high)
            if t == STEPS - 1:
                save(s).start()
            return 0

        def passage_now():
            return (power[0, slab], power[1, slab])

        def save(s):
            return pltpu.make_async_copy(
                field.at[s, :, pl.ds(HALO, slab)], out.at[:, s], out_sem.at[s]
            )

        lax.fori_loop(0, count, second_half, 0)

    for direction in range(2):
        @pl.when(has[direction])
        def _():
            side_copy(direction).wait_send()
            for s in range(count):
                halo_copy(s, direction).wait_send()
    for i, target in enumerate(owners):
        @pl.when(me != target)
        def _():
            pass_copy(i).wait_send()
    for t in range(STEPS):
        for chain in range(chains):
            @pl.when(me != owner(chain))
            def _():
                emit_copy(t, chain).wait_send()

            @pl.when(me == owner(chain))
            def _():
                def left(i, _):
                    scan_copy(t, chain // 2, chain % 2, lax.rem(me + i, n)).wait_send()
                    return 0

                lax.fori_loop(1, n, left, 0)
    for s in range(count):
        save(s).wait()


def local(n, sources, plan, absorb, labels, kk, damp, guess):
    count, slab, height, breadth = guess.shape[1:]
    chains = 2 * count
    slots = 1 if n >= chains else chains
    tile = (height, breadth)
    planes = slab + 2 * HALO
    f32 = jnp.float32
    dma = pltpu.SemaphoreType.DMA
    vmem = pl.BlockSpec(memory_space=pltpu.VMEM)
    smem = pl.BlockSpec(memory_space=pltpu.SMEM)
    hbm = pl.BlockSpec(memory_space=pl.ANY)
    owners = len({(c * n) // chains for c in range(chains)})
    scratch = [
        pltpu.VMEM((count, 2, planes) + tile, f32),
        pltpu.VMEM((count, 2, planes) + tile, f32),
        pltpu.VMEM((2, planes) + tile, f32),
        pltpu.VMEM((2, slab + 1) + tile, f32),
        pltpu.VMEM((2, 2, HALO - 1) + tile, f32),
        pltpu.VMEM((2, 2, HALO - 1) + tile, f32),
        pltpu.VMEM((2,) + tile, f32),
        pltpu.VMEM((2, 2) + tile, f32),
        pltpu.VMEM((STEPS, chains, 2) + tile, f32),
        pltpu.VMEM((STEPS, slots, n, 2) + tile, f32),
        pltpu.VMEM((STEPS, slots, n + 1, 2) + tile, f32),
        pltpu.VMEM((STEPS, count, 2, 2, 2) + tile, f32),
        pltpu.VMEM((n, 2) + tile, f32),
        dma((count,)),
        dma((count, 2)),
        dma((count, 2)),
        dma((2,)),
        dma((2,)),
        dma((owners,)),
        dma,
        dma((STEPS, chains)),
        dma((STEPS, slots)),
        dma((STEPS, slots, n)),
        dma((STEPS, count, 2)),
        dma((count,)),
    ]
    return pl.pallas_call(
        functools.partial(kernel, n, slots),
        out_shape=jax.ShapeDtypeStruct(guess.shape, f32),
        in_specs=[vmem, smem, vmem, vmem, smem, smem, hbm],
        out_specs=hbm,
        scratch_shapes=scratch,
        compiler_params=pltpu.CompilerParams(
            collective_id=0, has_side_effects=True, vmem_limit_bytes=48 * 2**20
        ),
        cost_estimate=pl.CostEstimate(
            flops=300 * guess.size, bytes_accessed=8 * guess.size, transcendentals=0
        ),
    )(sources, plan, absorb, labels, kk, damp, guess)


def solution(mesh):
    return jax.shard_map(
        functools.partial(local, mesh.shape["depth"]),
        mesh=mesh,
        in_specs=(
            P(None, "groups", None, None),
            P("groups"),
            P("depth", "groups", None),
            P("depth", "groups", None),
            P(),
            P("groups"),
            P(None, "groups", "depth", None, None),
        ),
        out_specs=P(None, "groups", "depth", None, None),
        check_vma=False,
    )
```

time: 242 us -> 60.2 us (0.25)
  the two profiles are of different devices: /device:TPU:25 before, /device:TPU:0 now
where the time goes in v1:
time: 60.2 us; the launch traced here: 59.9 us
  Pallas kernels  52.9 us (88%)
  local copies, waits for them, and re-layouts  7.01 us (12%)
    pallas_call x1, Pallas kernels, local(): pl.pallas_call(functools.partial(kernel, n, slots), out_shape=jax.ShapeDt...  52.9 us
    unnamed x15, local copies, waits for them, and re-layouts  7.01 us

profile of v1, /device:TPU:0, one launch (start us, length us, event | category | flops | bytes accessed | tf_op | source)
XLA Modules:
  0.0 59.9 jit_solution(14217115370823816065)
XLA Ops:
  0.0 0.0 copy-start
  0.0 1.6 %copy-done = f32[2,4,64,8,128]{4,3,2,1,0:T(8,128)S(1)} copy-done((f32[2,4,64,8,128]{4,3,2,1,0:T(8,128)S(1)}, f32[2,4,64,8,128]{4,3,2,1,0:T(8,128)}, u32[]{:S(2)}) %copy-start) | copy-done | bytes 2097176
  1.6 0.0 copy-start.1
  1.6 0.8 %copy-done.1 = f32[2,4,8,128]{3,2,1,0:T(8,128)S(1)} copy-done((f32[2,4,8,128]{3,2,1,0:T(8,128)S(1)}, f32[2,4,8,128]{3,2,1,0:T(8,128)}, u32[]{:S(2)}) %copy-start.1) | copy-done | bytes 32792
  2.4 0.0 copy-start.2
  2.4 0.7 %copy-done.2 = f32[1,8,128]{2,1,0:T(8,128)S(1)} copy-done((f32[1,8,128]{2,1,0:T(8,128)S(1)}, f32[1,8,128]{2,1,0:T(8,128)}, u32[]{:S(2)}) %copy-start.2) | copy-done | bytes 4120
  3.0 0.0 copy-start.3
  3.0 0.7 %copy-done.3 = s32[1,8,128]{2,1,0:T(8,128)S(1)} copy-done((s32[1,8,128]{2,1,0:T(8,128)S(1)}, s32[1,8,128]{2,1,0:T(8,128)}, u32[]{:S(2)}) %copy-start.3) | copy-done | bytes 4120
  3.7 0.0 copy-start.4
  3.7 0.7 %copy-done.4 = s32[4]{0:T(128)S(1)} copy-done((s32[4]{0:T(128)S(1)}, s32[4]{0:T(128)}, u32[]{:S(2)}) %copy-start.4) | copy-done | bytes 40
  4.4 0.0 copy-start.5
  4.4 0.7 %copy-done.5 = f32[8]{0:T(128)S(1)} copy-done((f32[8]{0:T(128)S(1)}, f32[8]{0:T(128)}, u32[]{:S(2)}) %copy-start.5) | copy-done | bytes 56
  5.0 0.0 copy-start.6
  5.0 0.7 %copy-done.6 = s32[128]{0:T(128)S(1)} copy-done((s32[128]{0:T(128)S(1)}, s32[128]{0:T(128)}, u32[]{:S(2)}) %copy-start.6) | copy-done | bytes 536
  5.7 52.9 %shard_map.73 = f32[2,4,64,8,128]{4,3,2,1,0:T(8,128)S(1)} custom-call(f32[2,4,8,128]{3,2,1,0:T(8,128)S(1)} %copy-done.1, s32[4]{0:T(128)S(1)} %copy-done.4, f32[1,8,128]{2,1,0:T(8,128)S(1)} %copy-done.2, s32[1,8,128]{2,1,0:T(8,128)S(1)} %copy-done.3, f32[8]{0:T(128)S(1)} %copy-done.5, s32[128]{0:T(128)S(1)} %copy-done.6, f32[2,4,64,8,128]{4,3,2,1,0:T(8,128)S(1)} %copy-done), custom_call_target="tpu_custom_call" | custom-call | flops 157286400 | bytes 4194304 | tf_op jit(solution)/shard_map/pallas_call | solution.py:501
  58.6 1.3 %copy.9 = f32[2,4,64,8,128]{4,3,2,1,0:T(8,128)} copy(f32[2,4,64,8,128]{4,3,2,1,0:T(8,128)S(1)} %shard_map.73) | data formatting | bytes 4194304
Async XLA Ops:
  0.0 1.6 %copy-start = (f32[2,4,64,8,128]{4,3,2,1,0:T(8,128)S(1)}, f32[2,4,64,8,128]{4,3,2,1,0:T(8,128)}, u32[]{:S(2)}) copy-start(f32[2,4,64,8,128]{4,3,2,1,0:T(8,128)} %guess.1) | copy-start | bytes 6291460
  1.6 0.8 %copy-start.1 = (f32[2,4,8,128]{3,2,1,0:T(8,128)S(1)}, f32[2,4,8,128]{3,2,1,0:T(8,128)}, u32[]{:S(2)}) copy-start(f32[2,4,8,128]{3,2,1,0:T(8,128)} %sources.1) | copy-start | bytes 98308
  2.4 0.7 %copy-start.2 = (f32[1,8,128]{2,1,0:T(8,128)S(1)}, f32[1,8,128]{2,1,0:T(8,128)}, u32[]{:S(2)}) copy-start(f32[1,8,128]{2,1,0:T(8,128)} %absorb.1) | copy-start | bytes 12292
  3.0 0.7 %copy-start.3 = (s32[1,8,128]{2,1,0:T(8,128)S(1)}, s32[1,8,128]{2,1,0:T(8,128)}, u32[]{:S(2)}) copy-start(s32[1,8,128]{2,1,0:T(8,128)} %labels.1) | copy-start | bytes 12292
  3.7 0.7 %copy-start.4 = (s32[4]{0:T(128)S(1)}, s32[4]{0:T(128)}, u32[]{:S(2)}) copy-start(s32[4]{0:T(128)} %plan.1) | copy-start | bytes 52
  4.4 0.7 %copy-start.5 = (f32[8]{0:T(128)S(1)}, f32[8]{0:T(128)}, u32[]{:S(2)}) copy-start(f32[8]{0:T(128)} %kk.1) | copy-start | bytes 100
  5.0 0.7 %copy-start.6 = (s32[128]{0:T(128)S(1)}, s32[128]{0:T(128)}, u32[]{:S(2)}) copy-start(s32[128]{0:T(128)} %damp.1) | copy-start | bytes 1540

commit v2 on v1

--- a/solution.py
+++ b/solution.py
@@ -9,7 +9,7 @@
 
 STEPS = 2
 HALO = 3 * STEPS
-CHUNK = 8
+CHUNK = 16
 
 relax_weight = 0.8
 shift_ratio = 0.5
@@ -26,9 +26,9 @@
 
 
 def kernel(
-    n, chains_of, sources, plan, absorb, labels, kk, damp, guess, out,
+    n, chains_of, sources_in, plan_in, absorb_in, labels_in, kk_in, damp_in, guess, out,
     field, work, inner, power, side_next, side_prev, own, side, emits, gathered, scanned,
-    incoming, passages, local_sem, halo_send, halo_recv, side_send, side_recv, pass_send,
+    incoming, passages, sources, plan, absorb, labels, kk, damp, arg_sem, local_sem, halo_send, halo_recv, side_send, side_recv, pass_send,
     pass_recv, emit_send, emit_recv, scan_send, scan_recv, out_sem,
 ):
     me = lax.axis_index("depth")
@@ -62,8 +62,21 @@
             guess.at[:, s], field.at[s, :, pl.ds(HALO, slab)], local_sem.at[s]
         )
 
+    fetches = [
+        pltpu.make_async_copy(there, here, arg_sem.at[i])
+        for i, (there, here) in enumerate(
+            (
+                (labels_in, labels), (kk_in, kk), (damp_in, damp), (absorb_in, absorb),
+                (plan_in, plan), (sources_in, sources),
+            )
+        )
+    ]
+    for fetch in fetches:
+        fetch.start()
     for s in range(count):
         load(s).start()
+    for fetch in fetches:
+        fetch.wait()
 
     label = labels[0]
     squared = jnp.zeros((height, breadth), jnp.float32)
@@ -221,6 +234,7 @@
         win = window(field, (s,), first + HALO, planes)
         source = (sources[0, s], sources[1, s])
         spot = plan[s] - me * slab
+        results = []
         for j in range(planes):
             value = (win[0][j + 1], win[1][j + 1])
             near = beside(win, j)
@@ -229,8 +243,7 @@
                 hit * source[0] + (near[0] - real * value[0] + damped * value[1]),
                 hit * source[1] + (near[1] - real * value[1] - damped * value[0]),
             )
-            work[s, 0, first + HALO + j] = res[0]
-            work[s, 1, first + HALO + j] = res[1]
+            results.append(res)
             if tally is not None:
                 forward, backward = tally
                 forward = cadd(cmul(a_own, forward), res)
@@ -238,34 +251,52 @@
                     backward, cmul((power[0, first + j], power[1, first + j]), res)
                 )
                 tally = (forward, backward)
+        for j in range(planes):
+            for c in range(2):
+                work[s, c, first + HALO + j] = results[j][c]
         return tally
 
     def start_pass(s, first, planes, g, toward, from_low, from_high):
-        for j in range(planes):
-            at = first + HALO + j
+        lead = first + HALO
+        held = [(work[s, 0, lead + j], work[s, 1, lead + j]) for j in range(planes)]
+        results = []
+        for j in range(planes):
             up, down = toward(first + j)
-            c = cadd(
-                (work[s, 0, at], work[s, 1, at]), cadd(cmul(up, from_low), cmul(down, from_high))
+            c = cadd(held[j], cadd(cmul(up, from_low), cmul(down, from_high)))
+            results.append(cmul(g, c))
+        for j in range(planes):
+            work[s, 0, lead + j], work[s, 1, lead + j] = results[j]
+
+    def middle_pass(s, first, planes, g):
+        lead = first + HALO
+        win = window(work, (s,), lead, planes)
+        results = []
+        for j in range(planes):
+            moved = cmul(g, beside(win, j))
+            results.append(
+                [(2.0 - relax_weight) * win[c][j + 1] + moved[c] for c in range(2)]
             )
-            work[s, 0, at], work[s, 1, at] = cmul(g, c)
-
-    def middle_pass(s, first, planes, g):
-        win = window(work, (s,), first + HALO, planes)
-        for j in range(planes):
-            at = first + HALO + j
+        for j in range(planes):
+            inner[0, lead + j], inner[1, lead + j] = results[j]
+
+    def last_pass(s, first, planes, g):
+        lead = first + HALO
+        win = window(inner, (), lead, planes)
+        held = [
+            [field[s, c, lead + j] + work[s, c, lead + j] for c in range(2)]
+            for j in range(planes)
+        ]
+        results = []
+        for j in range(planes):
             moved = cmul(g, beside(win, j))
-            for c in range(2):
-                inner[c, at] = (2.0 - relax_weight) * win[c][j + 1] + moved[c]
-
-    def last_pass(s, first, planes, g):
-        win = window(inner, (), first + HALO, planes)
-        for j in range(planes):
-            at = first + HALO + j
-            moved = cmul(g, beside(win, j))
-            for c in range(2):
-                field[s, c, at] = field[s, c, at] + (
-                    (1.0 - relax_weight) * win[c][j + 1] + work[s, c, at] + moved[c]
-                )
+            results.append(
+                [
+                    held[j][c] + ((1.0 - relax_weight) * win[c][j + 1] + moved[c])
+                    for c in range(2)
+                ]
+            )
+        for j in range(planes):
+            field[s, 0, lead + j], field[s, 1, lead + j] = results[j]
 
     def emit_copy(t, chain):
         return remote(
@@ -467,8 +498,6 @@
     planes = slab + 2 * HALO
     f32 = jnp.float32
     dma = pltpu.SemaphoreType.DMA
-    vmem = pl.BlockSpec(memory_space=pltpu.VMEM)
-    smem = pl.BlockSpec(memory_space=pltpu.SMEM)
     hbm = pl.BlockSpec(memory_space=pl.ANY)
     owners = len({(c * n) // chains for c in range(chains)})
     scratch = [
@@ -485,6 +514,13 @@
         pltpu.VMEM((STEPS, slots, n + 1, 2) + tile, f32),
         pltpu.VMEM((STEPS, count, 2, 2, 2) + tile, f32),
         pltpu.VMEM((n, 2) + tile, f32),
+        pltpu.VMEM(sources.shape, f32),
+        pltpu.SMEM(plan.shape, jnp.int32),
+        pltpu.VMEM(absorb.shape, f32),
+        pltpu.VMEM(labels.shape, jnp.int32),
+        pltpu.SMEM(kk.shape, f32),
+        pltpu.SMEM(damp.shape, jnp.int32),
+        dma((6,)),
         dma((count,)),
         dma((count, 2)),
         dma((count, 2)),
@@ -501,11 +537,11 @@
     return pl.pallas_call(
         functools.partial(kernel, n, slots),
         out_shape=jax.ShapeDtypeStruct(guess.shape, f32),
-        in_specs=[vmem, smem, vmem, vmem, smem, smem, hbm],
+        in_specs=[hbm] * 7,
         out_specs=hbm,
         scratch_shapes=scratch,
         compiler_params=pltpu.CompilerParams(
-            collective_id=0, has_side_effects=True, vmem_limit_bytes=48 * 2**20
+            collective_id=0, has_side_effects=True, vmem_limit_bytes=60 * 2**20
         ),
         cost_estimate=pl.CostEstimate(
             flops=300 * guess.size, bytes_accessed=8 * guess.size, transcendentals=0

time: 60.2 us -> 52.1 us (0.87)
  Pallas kernels: 52.9 us -> 48.8 us
  local copies, waits for them, and re-layouts: 7.01 us -> 3.06 us
    pallas_call x1, Pallas kernels: 52.9 us -> 48.8 us  [local(): pl.pallas_call(functools.partial(kernel, n, slots), out_shape=jax.ShapeDt...]
    unnamed x15 -> x1, local copies, waits for them, and re-layouts: 7.01 us -> 3.06 us
where the time goes in v2:
time: 52.1 us; the launch traced here: 51.9 us
  Pallas kernels  48.8 us (94%)
  local copies, waits for them, and re-layouts  3.06 us (6%)
    pallas_call x1, Pallas kernels, local(): pl.pallas_call(functools.partial(kernel, n, slots), out_shape=jax.ShapeDt...  48.8 us
    unnamed x1, local copies, waits for them, and re-layouts  3.06 us

profile of v2, /device:TPU:0, one launch (start us, length us, event | category | flops | bytes accessed | tf_op | source)
XLA Modules:
  0.0 51.9 jit_solution(7828398858081403267)
XLA Ops:
  0.0 48.8 %shard_map.73 = f32[2,4,64,8,128]{4,3,2,1,0:T(8,128)} custom-call(f32[2,4,8,128]{3,2,1,0:T(8,128)} %sources_in.1, s32[4]{0:T(128)} %plan_in.1, f32[1,8,128]{2,1,0:T(8,128)} %absorb_in.1, s32[1,8,128]{2,1,0:T(8,128)} %labels_in.1, f32[8]{0:T(128)} %kk_in.1, s32[128]{0:T(128)} %damp_in.1, f32[2,4,64,8,128]{4,3,2,1,0:T(8,128)} %guess.1), custom_call_target="tpu_custom_call" | custom-call | flops 157286400 | bytes 4194304 | tf_op jit(solution)/shard_map/pallas_call | solution.py:537
  48.9 3.1 %copy.9 = f32[2,4,64,8,128]{4,3,2,1,0:T(8,128)} copy(f32[2,4,64,8,128]{4,3,2,1,0:T(8,128)} %shard_map.73) | data formatting | bytes 4194304

commit v3 on v2

--- a/solution.py
+++ b/solution.py
@@ -9,7 +9,7 @@
 
 STEPS = 2
 HALO = 3 * STEPS
-CHUNK = 16
+CHUNK = 32
 
 relax_weight = 0.8
 shift_ratio = 0.5
@@ -29,7 +29,7 @@
     n, chains_of, sources_in, plan_in, absorb_in, labels_in, kk_in, damp_in, guess, out,
     field, work, inner, power, side_next, side_prev, own, side, emits, gathered, scanned,
     incoming, passages, sources, plan, absorb, labels, kk, damp, arg_sem, local_sem, halo_send, halo_recv, side_send, side_recv, pass_send,
-    pass_recv, emit_send, emit_recv, scan_send, scan_recv, out_sem,
+    pass_recv, emit_send, emit_recv, scan_send, scan_recv,
 ):
     me = lax.axis_index("depth")
     count = guess.shape[1]
@@ -230,73 +230,82 @@
     def beside(win, j):
         return tuple(w[j] + w[j + 2] + lateral(w[j + 1]) for w in win)
 
-    def residual_pass(s, first, planes, real, tally):
-        win = window(field, (s,), first + HALO, planes)
+    def residual_pass(s, parts, tally):
+        wins = [window(field, (s,), part[0] + HALO, part[1]) for part in parts]
         source = (sources[0, s], sources[1, s])
         spot = plan[s] - me * slab
         results = []
-        for j in range(planes):
-            value = (win[0][j + 1], win[1][j + 1])
-            near = beside(win, j)
-            hit = jnp.where(spot == first + j, 1.0, 0.0)
-            res = (
-                hit * source[0] + (near[0] - real * value[0] + damped * value[1]),
-                hit * source[1] + (near[1] - real * value[1] - damped * value[0]),
-            )
-            results.append(res)
-            if tally is not None:
-                forward, backward = tally
-                forward = cadd(cmul(a_own, forward), res)
-                backward = cadd(
-                    backward, cmul((power[0, first + j], power[1, first + j]), res)
+        for (first, planes, real), win in zip(parts, wins):
+            for j in range(planes):
+                value = (win[0][j + 1], win[1][j + 1])
+                near = beside(win, j)
+                hit = jnp.where(spot == first + j, 1.0, 0.0)
+                res = (
+                    hit * source[0] + (near[0] - real * value[0] + damped * value[1]),
+                    hit * source[1] + (near[1] - real * value[1] - damped * value[0]),
                 )
-                tally = (forward, backward)
-        for j in range(planes):
-            for c in range(2):
-                work[s, c, first + HALO + j] = results[j][c]
+                results.append((first + HALO + j, res))
+                if tally is not None:
+                    k = first + j
+                    ahead = (power[0, slab - 1 - k], power[1, slab - 1 - k])
+                    behind = (power[0, k], power[1, k])
+                    tally = (
+                        cadd(tally[0], cmul(ahead, res)), cadd(tally[1], cmul(behind, res))
+                    )
+        for at, res in results:
+            work[s, 0, at], work[s, 1, at] = res
         return tally
 
-    def start_pass(s, first, planes, g, toward, from_low, from_high):
-        lead = first + HALO
-        held = [(work[s, 0, lead + j], work[s, 1, lead + j]) for j in range(planes)]
+    def start_pass(s, parts):
         results = []
-        for j in range(planes):
-            up, down = toward(first + j)
-            c = cadd(held[j], cadd(cmul(up, from_low), cmul(down, from_high)))
-            results.append(cmul(g, c))
-        for j in range(planes):
-            work[s, 0, lead + j], work[s, 1, lead + j] = results[j]
-
-    def middle_pass(s, first, planes, g):
-        lead = first + HALO
-        win = window(work, (s,), lead, planes)
+        for first, planes, g, toward, from_low, from_high in parts:
+            for j in range(planes):
+                at = first + HALO + j
+                up, down = toward(first + j)
+                c = cadd(
+                    (work[s, 0, at], work[s, 1, at]),
+                    cadd(cmul(up, from_low), cmul(down, from_high)),
+                )
+                results.append((at, cmul(g, c)))
+        for at, value in results:
+            work[s, 0, at], work[s, 1, at] = value
+
+    def middle_pass(s, parts):
+        wins = [window(work, (s,), part[0] + HALO, part[1]) for part in parts]
         results = []
-        for j in range(planes):
-            moved = cmul(g, beside(win, j))
-            results.append(
-                [(2.0 - relax_weight) * win[c][j + 1] + moved[c] for c in range(2)]
-            )
-        for j in range(planes):
-            inner[0, lead + j], inner[1, lead + j] = results[j]
-
-    def last_pass(s, first, planes, g):
-        lead = first + HALO
-        win = window(inner, (), lead, planes)
-        held = [
-            [field[s, c, lead + j] + work[s, c, lead + j] for c in range(2)]
-            for j in range(planes)
-        ]
+        for (first, planes, g), win in zip(parts, wins):
+            for j in range(planes):
+                moved = cmul(g, beside(win, j))
+                results.append(
+                    (
+                        first + HALO + j,
+                        [(2.0 - relax_weight) * win[c][j + 1] + moved[c] for c in range(2)],
+                    )
+                )
+        for at, value in results:
+            inner[0, at], inner[1, at] = value
+
+    def last_pass(s, parts, final):
+        wins = [window(inner, (), part[0] + HALO, part[1]) for part in parts]
         results = []
-        for j in range(planes):
-            moved = cmul(g, beside(win, j))
-            results.append(
-                [
-                    held[j][c] + ((1.0 - relax_weight) * win[c][j + 1] + moved[c])
-                    for c in range(2)
-                ]
-            )
-        for j in range(planes):
-            field[s, 0, lead + j], field[s, 1, lead + j] = results[j]
+        for (first, planes, g), win in zip(parts, wins):
+            for j in range(planes):
+                at = first + HALO + j
+                moved = cmul(g, beside(win, j))
+                results.append(
+                    (
+                        first + j,
+                        [
+                            (field[s, c, at] + work[s, c, at])
+                            + ((1.0 - relax_weight) * win[c][j + 1] + moved[c])
+                            for c in range(2)
+                        ],
+                    )
+                )
+        for at, value in results:
+            field[s, 0, at + HALO], field[s, 1, at + HALO] = value
+            if final:
+                out[0, s, at], out[1, s, at] = value
 
     def emit_copy(t, chain):
         return remote(
@@ -346,122 +355,150 @@
                 incoming[t, s, direction] = scanned[t, here, pl.ds(me, 2)]
 
     pieces = slab // CHUNK
-    for t in range(STEPS):
-        reach = 3 * (STEPS - t)
-
-        def first_half(s, _):
-            if t == 0:
-                load(s).wait()
-                for direction in range(2):
-                    @pl.when(has[direction])
-                    def _():
-                        halo_copy(s, 1 - direction).wait_recv()
-            zero = jnp.zeros((height, breadth), jnp.float32)
-            tally = lax.fori_loop(
-                0, pieces,
-                lambda i, tally: residual_pass(s, i * CHUNK, CHUNK, real_own, tally),
-                ((zero, zero), (zero, zero)),
+    units = STEPS * count
+
+    def at_step(t, body):
+        for step in range(STEPS):
+            @pl.when(t == step)
+            def _():
+                body(3 * (STEPS - step))
+
+    def first_half(t, s):
+        @pl.when(t == 0)
+        def _():
+            load(s).wait()
+            for direction in range(2):
+                @pl.when(has[direction])
+                def _():
+                    halo_copy(s, 1 - direction).wait_recv()
+
+        zero = jnp.zeros((height, breadth), jnp.float32)
+        tally = lax.fori_loop(
+            0, pieces,
+            lambda i, tally: residual_pass(s, [(i * CHUNK, CHUNK, real_own)], tally),
+            ((zero, zero), (zero, zero)),
+        )
+        for direction in range(2):
+            chain = 2 * s + direction
+            emits[t, chain, 0], emits[t, chain, 1] = tally[direction]
+
+            @pl.when(me != owner(chain))
+            def _():
+                emit_copy(t, chain).start()
+
+            @pl.when(me == owner(chain))
+            def _():
+                gathered[t, slot(chain), me, 0] = tally[direction][0]
+                gathered[t, slot(chain), me, 1] = tally[direction][1]
+
+        def sides(reach):
+            residual_pass(
+                s, [(1 - reach, reach - 1, media[0][0]), (slab, reach - 1, media[1][0])], None
             )
-            for direction in range(2):
-                chain = 2 * s + direction
-                emits[t, chain, 0], emits[t, chain, 1] = tally[direction]
-
-                @pl.when(me != owner(chain))
-                def _():
-                    emit_copy(t, chain).start()
-
-                @pl.when(me == owner(chain))
-                def _():
-                    gathered[t, slot(chain), me, 0] = tally[direction][0]
-                    gathered[t, slot(chain), me, 1] = tally[direction][1]
-            residual_pass(s, 1 - reach, reach - 1, media[0][0], None)
-            residual_pass(s, slab, reach - 1, media[1][0], None)
-
-            @pl.when(s > 0)
-            def _():
-                own_scan_or_first(t, s - 1)
-            return 0
-
-        def own_scan_or_first(t, s):
-            if t == 0:
-                @pl.when(s == 0)
-                def _():
-                    for target in owners:
-                        @pl.when(me == target)
-                        def _():
-                            if n > 1:
-                                every = passages.at[pl.ds(0, n - 1)]
-                                pltpu.make_async_copy(every, every, pass_recv).wait()
-            own_scan(t, s)
-
-        lax.fori_loop(0, count, first_half, 0)
-        own_scan_or_first(t, jnp.int32(count - 1))
-
-        def second_half(s, _):
-            for direction in range(2):
-                @pl.when(me != owner(2 * s + direction))
-                def _():
-                    scan_copy(t, s, direction, me).wait_recv()
-
-            def arrived(direction, i):
-                return (incoming[t, s, direction, i, 0], incoming[t, s, direction, i, 1])
-
-            def emitted(direction):
-                return (emits[t, 2 * s + direction, 0], emits[t, 2 * s + direction, 1])
-
-            def scaled(z):
-                return (coupling * z[0], coupling * z[1])
-
-            next_low, next_own = arrived(0, 0), arrived(0, 1)
-            prev_own, prev_high = arrived(1, 0), arrived(1, 1)
-            next_high = scaled(cadd(cmul(passage_now(), next_own), emitted(0)))
-            prev_low = scaled(cadd(cmul(passage_now(), prev_own), emitted(1)))
-            next_low, next_own = scaled(next_low), scaled(next_own)
-            prev_own, prev_high = scaled(prev_own), scaled(prev_high)
-
-            def toward_own(k):
+
+        at_step(t, sides)
+
+    def passages_here():
+        for target in owners:
+            @pl.when(me == target)
+            def _():
+                if n > 1:
+                    every = passages.at[pl.ds(0, n - 1)]
+                    pltpu.make_async_copy(every, every, pass_recv).wait()
+
+    def second_half(t, s):
+        for direction in range(2):
+            @pl.when(me != owner(2 * s + direction))
+            def _():
+                scan_copy(t, s, direction, me).wait_recv()
+
+        def arrived(direction, i):
+            return (incoming[t, s, direction, i, 0], incoming[t, s, direction, i, 1])
+
+        def emitted(direction):
+            return (emits[t, 2 * s + direction, 0], emits[t, 2 * s + direction, 1])
+
+        def scaled(z):
+            return (coupling * z[0], coupling * z[1])
+
+        through = (power[0, slab], power[1, slab])
+        next_low, next_own = arrived(0, 0), arrived(0, 1)
+        prev_own, prev_high = arrived(1, 0), arrived(1, 1)
+        next_high = scaled(cadd(cmul(through, next_own), emitted(0)))
+        prev_low = scaled(cadd(cmul(through, prev_own), emitted(1)))
+        next_low, next_own = scaled(next_low), scaled(next_own)
+        prev_own, prev_high = scaled(prev_own), scaled(prev_high)
+
+        def toward_own(k):
+            return (
+                (power[0, k + 1], power[1, k + 1]),
+                (power[0, slab - k], power[1, slab - k]),
+            )
+
+        def toward_side(direction):
+            def get(k):
+                i = k - slab if direction else k + wing
                 return (
-                    (power[0, k + 1], power[1, k + 1]),
-                    (power[0, slab - k], power[1, slab - k]),
+                    (side_next[direction, 0, i], side_next[direction, 1, i]),
+                    (side_prev[direction, 0, i], side_prev[direction, 1, i]),
                 )
-
-            def toward_side(direction):
-                def get(k):
-                    i = k - slab if direction else k + wing
-                    return (
-                        (side_next[direction, 0, i], side_next[direction, 1, i]),
-                        (side_prev[direction, 0, i], side_prev[direction, 1, i]),
-                    )
-                return get
-
-            g_low, g_high = media[0][1], media[1][1]
-
-            def walk(body):
-                lax.fori_loop(0, pieces, lambda i, _: (body(i * CHUNK), 0)[1], 0)
-
-            walk(lambda k: start_pass(s, k, CHUNK, g_own, toward_own, next_own, prev_own))
-            start_pass(s, 1 - reach, reach - 1, g_low, toward_side(0), next_low, prev_low)
-            start_pass(s, slab, reach - 1, g_high, toward_side(1), next_high, prev_high)
-            walk(lambda k: middle_pass(s, k, CHUNK, g_own))
-            middle_pass(s, 2 - reach, reach - 2, g_low)
-            middle_pass(s, slab, reach - 2, g_high)
-            walk(lambda k: last_pass(s, k, CHUNK, g_own))
+            return get
+
+        g_low, g_high = media[0][1], media[1][1]
+
+        def walk(body):
+            lax.fori_loop(0, pieces, lambda i, _: (body(i * CHUNK), 0)[1], 0)
+
+        walk(
+            lambda k: start_pass(s, [(k, CHUNK, g_own, toward_own, next_own, prev_own)])
+        )
+
+        def start_sides(reach):
+            start_pass(
+                s,
+                [
+                    (1 - reach, reach - 1, g_low, toward_side(0), next_low, prev_low),
+                    (slab, reach - 1, g_high, toward_side(1), next_high, prev_high),
+                ],
+            )
+            middle_pass(s, [(2 - reach, reach - 2, g_low), (slab, reach - 2, g_high)])
+
+        at_step(t, start_sides)
+        walk(lambda k: middle_pass(s, [(k, CHUNK, g_own)]))
+        walk(lambda k: last_pass(s, [(k, CHUNK, g_own)], True))
+
+        def last_sides(reach):
             if reach > 3:
-                last_pass(s, 3 - reach, reach - 3, g_low)
-                last_pass(s, slab, reach - 3, g_high)
-            if t == STEPS - 1:
-                save(s).start()
-            return 0
-
-        def passage_now():
-            return (power[0, slab], power[1, slab])
-
-        def save(s):
-            return pltpu.make_async_copy(
-                field.at[s, :, pl.ds(HALO, slab)], out.at[:, s], out_sem.at[s]
-            )
-
-        lax.fori_loop(0, count, second_half, 0)
+                last_pass(
+                    s, [(3 - reach, reach - 3, g_low), (slab, reach - 3, g_high)], False
+                )
+
+        at_step(t, last_sides)
+
+    def tick(i, _):
+        late = i - count
+
+        @pl.when(late >= 0)
+        def _():
+            second_half(late // count, late % count)
+
+        @pl.when(i < units)
+        def _():
+            first_half(i // count, i % count)
+
+        scan = i - 2
+
+        @pl.when(scan == 0)
+        def _():
+            passages_here()
+
+        @pl.when(jnp.logical_and(scan >= 0, scan < units))
+        def _():
+            own_scan(scan // count, scan % count)
+
+        return 0
+
+    lax.fori_loop(0, units + count, tick, 0)
 
     for direction in range(2):
         @pl.when(has[direction])
@@ -486,8 +523,6 @@
                     return 0
 
                 lax.fori_loop(1, n, left, 0)
-    for s in range(count):
-        save(s).wait()
 
 
 def local(n, sources, plan, absorb, labels, kk, damp, guess):
@@ -498,7 +533,7 @@
     planes = slab + 2 * HALO
     f32 = jnp.float32
     dma = pltpu.SemaphoreType.DMA
-    hbm = pl.BlockSpec(memory_space=pl.ANY)
+    hbm = pl.BlockSpec(memory_space=pltpu.HBM)
     owners = len({(c * n) // chains for c in range(chains)})
     scratch = [
         pltpu.VMEM((count, 2, planes) + tile, f32),
@@ -532,13 +567,12 @@
         dma((STEPS, slots)),
         dma((STEPS, slots, n)),
         dma((STEPS, count, 2)),
-        dma((count,)),
     ]
     return pl.pallas_call(
         functools.partial(kernel, n, slots),
         out_shape=jax.ShapeDtypeStruct(guess.shape, f32),
         in_specs=[hbm] * 7,
-        out_specs=hbm,
+        out_specs=pl.BlockSpec(memory_space=pltpu.VMEM),
         scratch_shapes=scratch,
         compiler_params=pltpu.CompilerParams(
             collective_id=0, has_side_effects=True, vmem_limit_bytes=60 * 2**20

time: 52.1 us -> 48.8 us (0.937)
  Pallas kernels: 48.8 us -> 45.5 us
    pallas_call x1, Pallas kernels: 48.8 us -> 45.5 us  [local(): pl.pallas_call(functools.partial(kernel, n, slots), out_shape=jax.ShapeDt...]
where the time goes in v3:
time: 48.8 us; the launch traced here: 48.6 us
  Pallas kernels  45.5 us (93%)
  local copies, waits for them, and re-layouts  3.06 us (6%)
    pallas_call x1, Pallas kernels, local(): pl.pallas_call(functools.partial(kernel, n, slots), out_shape=jax.ShapeDt...  45.5 us
    unnamed x1, local copies, waits for them, and re-layouts  3.06 us

profile of v3, /device:TPU:0, one launch (start us, length us, event | category | flops | bytes accessed | tf_op | source)
XLA Modules:
  0.0 48.6 jit_solution(5340540668255572689)
XLA Ops:
  0.0 45.5 %shard_map.73 = f32[2,4,64,8,128]{4,3,2,1,0:T(8,128)} custom-call(f32[2,4,8,128]{3,2,1,0:T(8,128)} %sources_in.1, s32[4]{0:T(128)} %plan_in.1, f32[1,8,128]{2,1,0:T(8,128)} %absorb_in.1, s32[1,8,128]{2,1,0:T(8,128)} %labels_in.1, f32[8]{0:T(128)} %kk_in.1, s32[128]{0:T(128)} %damp_in.1, f32[2,4,64,8,128]{4,3,2,1,0:T(8,128)} %guess.1), custom_call_target="tpu_custom_call" | custom-call | flops 157286400 | bytes 4194304 | tf_op jit(solution)/shard_map/pallas_call | solution.py:571
  45.5 3.1 %copy.9 = f32[2,4,64,8,128]{4,3,2,1,0:T(8,128)} copy(f32[2,4,64,8,128]{4,3,2,1,0:T(8,128)} %shard_map.73) | data formatting | bytes 4194304

commit v4 on v3

--- a/solution.py
+++ b/solution.py
@@ -9,7 +9,7 @@
 
 STEPS = 2
 HALO = 3 * STEPS
-CHUNK = 32
+CHUNK = 16
 
 relax_weight = 0.8
 shift_ratio = 0.5
@@ -28,7 +28,7 @@
 def kernel(
     n, chains_of, sources_in, plan_in, absorb_in, labels_in, kk_in, damp_in, guess, out,
     field, work, inner, power, side_next, side_prev, own, side, emits, gathered, scanned,
-    incoming, passages, sources, plan, absorb, labels, kk, damp, arg_sem, local_sem, halo_send, halo_recv, side_send, side_recv, pass_send,
+    incoming, passages, pairing, sources, plan, absorb, labels, kk, damp, arg_sem, local_sem, halo_send, halo_recv, side_send, side_recv, pass_send,
     pass_recv, emit_send, emit_recv, scan_send, scan_recv,
 ):
     me = lax.axis_index("depth")
@@ -222,13 +222,42 @@
         right = jnp.where(keep_right, pltpu.roll(x, breadth - 1, 1), 0.0)
         return (up + down) + (left + right)
 
+    def vertical(x):
+        up = jnp.where(keep_up, pltpu.roll(x, 1, 0), 0.0)
+        down = jnp.where(keep_down, pltpu.roll(x, height - 1, 0), 0.0)
+        return up + down
+
+    gap = lax.broadcasted_iota(jnp.int32, (breadth, breadth), 0) - lax.broadcasted_iota(
+        jnp.int32, (breadth, breadth), 1
+    )
+    pairing[...] = jnp.where(jnp.logical_or(gap == 1, gap == -1), 1.0, 0.0).astype(
+        jnp.bfloat16
+    )
+
     def window(ref, lead, first, planes):
-        return [
+        tiles = [
             [ref[lead + (c, first - 1 + j)] for j in range(planes + 2)] for c in range(2)
         ]
+        if planes < CHUNK:
+            return [(tiles[c], None) for c in range(2)]
+        both = []
+        for c in range(2):
+            flat = ref[lead + (c, pl.ds(first, planes))].reshape(planes * height, breadth)
+            coarse = flat.astype(jnp.bfloat16)
+            fine = (flat - coarse.astype(jnp.float32)).astype(jnp.bfloat16)
+            total = jnp.dot(coarse, pairing[...], preferred_element_type=jnp.float32)
+            total += jnp.dot(fine, pairing[...], preferred_element_type=jnp.float32)
+            both.append(
+                (tiles[c], [total[j * height : (j + 1) * height] for j in range(planes)])
+            )
+        return both
 
     def beside(win, j):
-        return tuple(w[j] + w[j + 2] + lateral(w[j + 1]) for w in win)
+        return tuple(
+            w[j] + w[j + 2]
+            + (lateral(w[j + 1]) if pairs is None else vertical(w[j + 1]) + pairs[j])
+            for w, pairs in win
+        )
 
     def residual_pass(s, parts, tally):
         wins = [window(field, (s,), part[0] + HALO, part[1]) for part in parts]
@@ -237,7 +266,7 @@
         results = []
         for (first, planes, real), win in zip(parts, wins):
             for j in range(planes):
-                value = (win[0][j + 1], win[1][j + 1])
+                value = (win[0][0][j + 1], win[1][0][j + 1])
                 near = beside(win, j)
                 hit = jnp.where(spot == first + j, 1.0, 0.0)
                 res = (
@@ -279,7 +308,7 @@
                 results.append(
                     (
                         first + HALO + j,
-                        [(2.0 - relax_weight) * win[c][j + 1] + moved[c] for c in range(2)],
+                        [(2.0 - relax_weight) * win[c][0][j + 1] + moved[c] for c in range(2)],
                     )
                 )
         for at, value in results:
@@ -297,7 +326,7 @@
                         first + j,
                         [
                             (field[s, c, at] + work[s, c, at])
-                            + ((1.0 - relax_weight) * win[c][j + 1] + moved[c])
+                            + ((1.0 - relax_weight) * win[c][0][j + 1] + moved[c])
                             for c in range(2)
                         ],
                     )
@@ -549,6 +578,7 @@
         pltpu.VMEM((STEPS, slots, n + 1, 2) + tile, f32),
         pltpu.VMEM((STEPS, count, 2, 2, 2) + tile, f32),
         pltpu.VMEM((n, 2) + tile, f32),
+        pltpu.VMEM((breadth, breadth), jnp.bfloat16),
         pltpu.VMEM(sources.shape, f32),
         pltpu.SMEM(plan.shape, jnp.int32),
         pltpu.VMEM(absorb.shape, f32),

time: 48.8 us -> 53.9 us (1.10)
  Pallas kernels: 45.5 us -> 50.7 us
    pallas_call x1, Pallas kernels: 45.5 us -> 50.7 us  [local(): pl.pallas_call(functools.partial(kernel, n, slots), out_shape=jax.ShapeDt...]
where the time goes in v4:
time: 53.9 us; the launch traced here: 53.7 us
  Pallas kernels  50.7 us (94%)
  local copies, waits for them, and re-layouts  3.06 us (6%)
    pallas_call x1, Pallas kernels, local(): pl.pallas_call(functools.partial(kernel, n, slots), out_shape=jax.ShapeDt...  50.7 us
    unnamed x1, local copies, waits for them, and re-layouts  3.06 us

profile of v4, /device:TPU:0, one launch (start us, length us, event | category | flops | bytes accessed | tf_op | source)
XLA Modules:
  0.0 53.7 jit_solution(944332056350296925)
XLA Ops:
  0.0 50.7 %shard_map.73 = f32[2,4,64,8,128]{4,3,2,1,0:T(8,128)} custom-call(f32[2,4,8,128]{3,2,1,0:T(8,128)} %sources_in.1, s32[4]{0:T(128)} %plan_in.1, f32[1,8,128]{2,1,0:T(8,128)} %absorb_in.1, s32[1,8,128]{2,1,0:T(8,128)} %labels_in.1, f32[8]{0:T(128)} %kk_in.1, s32[128]{0:T(128)} %damp_in.1, f32[2,4,64,8,128]{4,3,2,1,0:T(8,128)} %guess.1), custom_call_target="tpu_custom_call" | custom-call | flops 157286400 | bytes 4194304 | tf_op jit(solution)/shard_map/pallas_call | solution.py:601
  50.7 3.1 %copy.9 = f32[2,4,64,8,128]{4,3,2,1,0:T(8,128)} copy(f32[2,4,64,8,128]{4,3,2,1,0:T(8,128)} %shard_map.73) | data formatting | bytes 4194304

commit v5 on v3

--- a/solution.py
+++ b/solution.py
@@ -9,7 +9,7 @@
 
 STEPS = 2
 HALO = 3 * STEPS
-CHUNK = 32
+CHUNK = 16
 
 relax_weight = 0.8
 shift_ratio = 0.5
@@ -223,9 +223,8 @@
         return (up + down) + (left + right)
 
     def window(ref, lead, first, planes):
-        return [
-            [ref[lead + (c, first - 1 + j)] for j in range(planes + 2)] for c in range(2)
-        ]
+        view = ref.at[lead + (slice(None), pl.ds(first - 1, planes + 2))]
+        return [[view[c, j] for j in range(planes + 2)] for c in range(2)]
 
     def beside(win, j):
         return tuple(w[j] + w[j + 2] + lateral(w[j + 1]) for w in win)
@@ -236,6 +235,10 @@
         spot = plan[s] - me * slab
         results = []
         for (first, planes, real), win in zip(parts, wins):
+            view = work.at[s, :, pl.ds(first + HALO, planes)]
+            if tally is not None:
+                far = power.at[:, pl.ds(slab - first - planes, planes)]
+                near_by = power.at[:, pl.ds(first, planes)]
             for j in range(planes):
                 value = (win[0][j + 1], win[1][j + 1])
                 near = beside(win, j)
@@ -244,68 +247,74 @@
                     hit * source[0] + (near[0] - real * value[0] + damped * value[1]),
                     hit * source[1] + (near[1] - real * value[1] - damped * value[0]),
                 )
-                results.append((first + HALO + j, res))
+                results.append((view, j, res))
                 if tally is not None:
-                    k = first + j
-                    ahead = (power[0, slab - 1 - k], power[1, slab - 1 - k])
-                    behind = (power[0, k], power[1, k])
+                    ahead = (far[0, planes - 1 - j], far[1, planes - 1 - j])
+                    behind = (near_by[0, j], near_by[1, j])
                     tally = (
                         cadd(tally[0], cmul(ahead, res)), cadd(tally[1], cmul(behind, res))
                     )
-        for at, res in results:
-            work[s, 0, at], work[s, 1, at] = res
+        for view, j, res in results:
+            view[0, j], view[1, j] = res
         return tally
 
     def start_pass(s, parts):
         results = []
         for first, planes, g, toward, from_low, from_high in parts:
+            view = work.at[s, :, pl.ds(first + HALO, planes)]
+            coefficient = toward(first, planes)
             for j in range(planes):
-                at = first + HALO + j
-                up, down = toward(first + j)
+                up, down = coefficient(j)
                 c = cadd(
-                    (work[s, 0, at], work[s, 1, at]),
+                    (view[0, j], view[1, j]),
                     cadd(cmul(up, from_low), cmul(down, from_high)),
                 )
-                results.append((at, cmul(g, c)))
-        for at, value in results:
-            work[s, 0, at], work[s, 1, at] = value
+                results.append((view, j, cmul(g, c)))
+        for view, j, value in results:
+            view[0, j], view[1, j] = value
 
     def middle_pass(s, parts):
         wins = [window(work, (s,), part[0] + HALO, part[1]) for part in parts]
         results = []
         for (first, planes, g), win in zip(parts, wins):
+            view = inner.at[:, pl.ds(first + HALO, planes)]
             for j in range(planes):
                 moved = cmul(g, beside(win, j))
                 results.append(
                     (
-                        first + HALO + j,
+                        view,
+                        j,
                         [(2.0 - relax_weight) * win[c][j + 1] + moved[c] for c in range(2)],
                     )
                 )
-        for at, value in results:
-            inner[0, at], inner[1, at] = value
+        for view, j, value in results:
+            view[0, j], view[1, j] = value
 
     def last_pass(s, parts, final):
         wins = [window(inner, (), part[0] + HALO, part[1]) for part in parts]
         results = []
         for (first, planes, g), win in zip(parts, wins):
+            view = field.at[s, :, pl.ds(first + HALO, planes)]
+            begun = work.at[s, :, pl.ds(first + HALO, planes)]
+            target = out.at[:, s, pl.ds(first, planes)] if final else None
             for j in range(planes):
-                at = first + HALO + j
                 moved = cmul(g, beside(win, j))
                 results.append(
                     (
-                        first + j,
+                        view,
+                        target,
+                        j,
                         [
-                            (field[s, c, at] + work[s, c, at])
+                            (view[c, j] + begun[c, j])
                             + ((1.0 - relax_weight) * win[c][j + 1] + moved[c])
                             for c in range(2)
                         ],
                     )
                 )
-        for at, value in results:
-            field[s, 0, at + HALO], field[s, 1, at + HALO] = value
+        for view, target, j, value in results:
+            view[0, j], view[1, j] = value
             if final:
-                out[0, s, at], out[1, s, at] = value
+                target[0, j], target[1, j] = value
 
     def emit_copy(t, chain):
         return remote(
@@ -429,18 +438,18 @@
         next_low, next_own = scaled(next_low), scaled(next_own)
         prev_own, prev_high = scaled(prev_own), scaled(prev_high)
 
-        def toward_own(k):
-            return (
-                (power[0, k + 1], power[1, k + 1]),
-                (power[0, slab - k], power[1, slab - k]),
-            )
+        def toward_own(first, planes):
+            up = power.at[:, pl.ds(first + 1, planes)]
+            down = power.at[:, pl.ds(slab - first - planes + 1, planes)]
+            back = planes - 1
+            return lambda j: ((up[0, j], up[1, j]), (down[0, back - j], down[1, back - j]))
 
         def toward_side(direction):
-            def get(k):
-                i = k - slab if direction else k + wing
-                return (
-                    (side_next[direction, 0, i], side_next[direction, 1, i]),
-                    (side_prev[direction, 0, i], side_prev[direction, 1, i]),
+            def get(first, planes):
+                i = first - slab if direction else first + wing
+                return lambda j: (
+                    (side_next[direction, 0, i + j], side_next[direction, 1, i + j]),
+                    (side_prev[direction, 0, i + j], side_prev[direction, 1, i + j]),
                 )
             return get
 

time: 48.8 us -> 50.5 us (1.035)
  Pallas kernels: 45.5 us -> 47.3 us
    pallas_call x1, Pallas kernels: 45.5 us -> 47.3 us  [local(): pl.pallas_call(functools.partial(kernel, n, slots), out_shape=jax.ShapeDt...]
where the time goes in v5:
time: 50.5 us; the launch traced here: 50.4 us
  Pallas kernels  47.3 us (94%)
  local copies, waits for them, and re-layouts  3.06 us (6%)
    pallas_call x1, Pallas kernels, local(): pl.pallas_call(functools.partial(kernel, n, slots), out_shape=jax.ShapeDt...  47.3 us
    unnamed x1, local copies, waits for them, and re-layouts  3.06 us

profile of v5, /device:TPU:0, one launch (start us, length us, event | category | flops | bytes accessed | tf_op | source)
XLA Modules:
  0.0 50.4 jit_solution(4138448869494805946)
XLA Ops:
  0.0 47.3 %shard_map.73 = f32[2,4,64,8,128]{4,3,2,1,0:T(8,128)} custom-call(f32[2,4,8,128]{3,2,1,0:T(8,128)} %sources_in.1, s32[4]{0:T(128)} %plan_in.1, f32[1,8,128]{2,1,0:T(8,128)} %absorb_in.1, s32[1,8,128]{2,1,0:T(8,128)} %labels_in.1, f32[8]{0:T(128)} %kk_in.1, s32[128]{0:T(128)} %damp_in.1, f32[2,4,64,8,128]{4,3,2,1,0:T(8,128)} %guess.1), custom_call_target="tpu_custom_call" | custom-call | flops 157286400 | bytes 4194304 | tf_op jit(solution)/shard_map/pallas_call | solution.py:580
  47.3 3.1 %copy.9 = f32[2,4,64,8,128]{4,3,2,1,0:T(8,128)} copy(f32[2,4,64,8,128]{4,3,2,1,0:T(8,128)} %shard_map.73) | data formatting | bytes 4194304
